TPU v7x, 512 devices: a whole 4x4x16 slice. The times are simulated.
512 devices in a mesh: img: 64 (over y, z_lo, x), tpl: 4 (over z_hi), pix: 2 (over core).
Axes of the slice: x: 4, y: 4, z: 16 (z_hi: 4, z_lo: 4; z = z_hi * 4 + z_lo), core: 2. Of those that a mesh axis runs over, the one named last changes fastest.
Arguments:
- images: bfloat16 [16384, 128, 128], P(('img', 'tpl'), 'pix'), may hold values from -6 to 6
- conformers: float32 [8, 3, 4096], replicated, may hold values from -96 to 96
- atom_types: int32 [4096], replicated, may hold values from 0 to 4
- type_amp: float32 [5], replicated, may hold values from 0.3 to 3
- type_width: float32 [5], replicated, may hold values from 0.8 to 2.5
- view_angles: float32 [256, 3], replicated, may hold values from -3.140625 to 3.140625
- template_conf: int32 [512], P(('tpl', 'img')), may hold values from 0 to 7
- template_view: int32 [512], P(('tpl', 'img')), may hold values from 0 to 255
- group_ids: int32 [16384], P('img'), may hold values from 0 to 255
- group_prec: float32 [256], replicated, may hold values from 0.3 to 45
Outputs:
- averages: float32 [512, 128, 128], P(('tpl', 'img'), 'pix')
- loglik: float32 [16384], P(('img', 'tpl'))
All inputs are finite; a program needn't handle non-finite values.
Results may differ from a plain program's by a relative error of at most 0.013.
Values may be sent and summed in bfloat16 or wider, within the bound.
A program may use at most 64 MiB of HBM per device.

v0:
```python
import jax
import jax.numpy as jnp
from jax import lax
from jax.sharding import PartitionSpec as P


def atom_tables(atom_types, type_amp, type_width):
    hits = atom_types[:, None] == jnp.arange(type_amp.shape[0], dtype=jnp.int32)[None, :]
    atom_amp = jnp.sum(jnp.where(hits, type_amp[None, :], 0.0), axis=1) * 0.0625
    widths = jnp.sum(jnp.where(hits, type_width[None, :], 0.0), axis=1)
    return (atom_amp, 0.5 / (widths * widths))


def view_rows(angles):
    cos_phi = jnp.cos(angles[0])
    sin_phi = jnp.sin(angles[0])
    cos_theta = jnp.cos(angles[1])
    sin_theta = jnp.sin(angles[1])
    cos_psi = jnp.cos(angles[2])
    sin_psi = jnp.sin(angles[2])
    first_row = (
        cos_phi * cos_theta * cos_psi - sin_phi * sin_psi,
        -cos_phi * cos_theta * sin_psi - sin_phi * cos_psi,
        cos_phi * sin_theta,
    )
    second_row = (
        sin_phi * cos_theta * cos_psi + cos_phi * sin_psi,
        -sin_phi * cos_theta * sin_psi + cos_phi * cos_psi,
        sin_phi * sin_theta,
    )
    return (first_row, second_row)


def render_one(coords, angles, atom_amp, inv_spread, row_pos, col_pos):
    first_row, second_row = view_rows(angles)
    across = first_row[0] * coords[0] + first_row[1] * coords[1] + first_row[2] * coords[2]
    down = second_row[0] * coords[0] + second_row[1] * coords[1] + second_row[2] * coords[2]
    col_table = jnp.exp(-jnp.square(col_pos[None, :] - across[:, None]) * inv_spread[:, None])
    row_table = atom_amp[:, None] * jnp.exp(
        -jnp.square(row_pos[None, :] - down[:, None]) * inv_spread[:, None]
    )
    return lax.dot_general(
        row_table,
        col_table,
        (((0,), (0,)), ((), ())),
        precision=lax.Precision.HIGHEST,
        preferred_element_type=jnp.float32,
    )


def group_lookup(group_ids, group_prec):
    hits = group_ids[:, None] == jnp.arange(group_prec.shape[0], dtype=jnp.int32)[None, :]
    return jnp.sum(jnp.where(hits, group_prec[None, :], 0.0), axis=1)


def on_device(
    images,
    conformers,
    atom_types,
    type_amp,
    type_width,
    view_angles,
    template_conf,
    template_view,
    group_ids,
    group_prec,
):
    img_dev, half_rows, side = images.shape
    pixel_count = half_rows * side
    flat_rows = images.reshape(img_dev, pixel_count)
    pix_index = lax.axis_index("pix")
    tpl_index = lax.axis_index("tpl")
    tpl_count = lax.axis_size("tpl")
    atom_amp, inv_spread = atom_tables(atom_types, type_amp, type_width)
    col_pos = jnp.arange(side).astype(jnp.float32) - side * 0.5 + 0.5
    row_pos = (
        (pix_index * half_rows + jnp.arange(half_rows, dtype=jnp.int32)).astype(jnp.float32)
        - side * 0.5
        + 0.5
    )
    own_coords = jnp.take(conformers, template_conf, axis=0)
    own_angles = jnp.take(view_angles, template_view, axis=0)
    own_rendered = jax.vmap(
        lambda coords, angles: render_one(coords, angles, atom_amp, inv_spread, row_pos, col_pos)
    )(own_coords, own_angles)
    rendered_count = own_rendered.shape[0]
    own_rendered = own_rendered.astype(jnp.bfloat16).reshape(rendered_count, pixel_count)
    templates = lax.all_gather(own_rendered, "img", axis=0, tiled=True)
    tpl_dev = templates.shape[0]
    part_norms = jnp.sum(jnp.square(templates.astype(jnp.float32)), axis=1)
    precision_rows = group_lookup(group_ids, group_prec)
    img_grp = precision_rows.shape[0]
    group_images = lax.all_gather(flat_rows, "tpl", axis=0, tiled=True)
    part_scores = lax.dot_general(
        group_images, templates, (((1,), (1,)), ((), ())), preferred_element_type=jnp.float32
    )
    anchor = jnp.zeros((), jnp.int32)
    score_block = lax.dynamic_update_slice(
        jnp.zeros((img_grp, tpl_dev * tpl_count), jnp.float32),
        part_scores,
        (anchor, tpl_index * tpl_dev),
    )
    norm_block = lax.dynamic_update_slice(
        jnp.zeros((tpl_dev * tpl_count,), jnp.float32), part_norms, (tpl_index * tpl_dev,)
    )
    full_scores, full_norms = lax.psum((score_block, norm_block), ("tpl", "pix"))
    logits = precision_rows[:, None] * full_scores * lax.rsqrt(full_norms + 1e-06)[None, :]
    maximum = jnp.max(logits, axis=1)
    weights = jnp.exp(logits - maximum[:, None])
    totals = jnp.sum(weights, axis=1)
    own_weights = lax.dynamic_slice_in_dim(weights, tpl_index * tpl_dev, tpl_dev, 1)
    resp = (own_weights / totals[:, None]).astype(jnp.bfloat16)
    loglik = maximum + jnp.log(totals)
    own_loglik = lax.dynamic_slice_in_dim(loglik, tpl_index * img_dev, img_dev, 0)
    own_sums = lax.psum_scatter(
        lax.dot_general(
            resp, group_images, (((0,), (0,)), ((), ())), preferred_element_type=jnp.float32
        ),
        "img",
        scatter_dimension=0,
        tiled=True,
    )
    part_squares = jnp.sum(jnp.square(own_sums), axis=1)
    full_squares = lax.psum(part_squares, "pix")
    scale = lax.rsqrt(full_squares / (side * side) + 1e-06)
    averages = (own_sums * scale[:, None]).reshape(rendered_count, half_rows, side)
    return (averages, own_loglik)


def solution(mesh):
    placed = (
        P(("img", "tpl"), "pix", None),
        P(),
        P(),
        P(),
        P(),
        P(),
        P(("tpl", "img")),
        P(("tpl", "img")),
        P("img"),
        P(),
    )
    return jax.shard_map(
        on_device,
        mesh=mesh,
        in_specs=placed,
        out_specs=(P(("tpl", "img"), "pix", None), P(("img", "tpl"))),
        check_vma=False,
    )
```

profile of v0, /device:TPU:1, one launch (start us, length us, event | category | flops | bytes accessed | tf_op | source)
XLA Modules:
  0.0 1392.9 jit_solution(15018643670695546310)
XLA Ops:
  7.2 0.7 compare_select_fusion
  7.9 0.7 compare_and_fusion
  8.6 0.8 copy.15
  9.5 0.6 gather_fusion
  10.1 0.3 add_reduce_fusion.1
  10.4 0.9 gather_fusion.1
  11.4 0.1 broadcast_select_fusion
  11.5 0.9 select_reduce_fusion.2
  12.4 0.1 multiply_add_fusion.1
  12.5 4.2 fusion.16
  16.7 0.6 reshape.202
  17.4 1.7 copy.20
  19.2 314.0 %all-gather.6.cloned.1.call-done = bf16[64,2,8192]{2,1,0:T(2,128)(2,1)} async-done(((bf16[1,2,8192]{2,1,0:T(2,128)(2,1)}), bf16[64,2,8192]{2,1,0:T(2,128)(2,1)}) %all-gather.6.cloned.1.call-update) | async-done | bytes 2097168 | tf_op jit(solution)/shard_map/all_gather | solution.py:88
  333.2 2.7 reshape.203
  336.0 204.9 %all-gather.4.cloned.1.call-done = bf16[256,8192]{1,0:T(8,128)(2,1)} async-done(((bf16[64,8192]{1,0:T(8,128)(2,1)}), bf16[256,8192]{1,0:T(8,128)(2,1)}) %all-gather.4.cloned.1.call-update) | async-done | bytes 4194320 | tf_op jit(solution)/shard_map/all_gather | solution.py:93
  540.9 3.7 fusion.15
  544.7 0.8 copy-done.1
  545.6 0.2 select_reduce_fusion
  545.7 0.5 multiply_reduce_fusion
  546.2 0.2 dynamic_update_slice.7
  546.5 18.4 %psum.22 = f32[512]{0:T(512)S(1)} all-reduce(f32[512]{0:T(512)S(1)} %dynamic_update_slice.7), channel_id=1, replica_groups=mesh['img'=64,'tpl'=4,'pix'=2] {'tpl','pix'}, use_global_device_ids=true, to_apply=%region_5.6 | all-reduce | flops 512 | bytes 4096 | tf_op jit(solution)/shard_map/psum | solution.py:106
  564.8 77.6 %all-reduce.4.cloned.1.call-done = f32[256,512]{0,1:T(8,128)} async-done(((f32[256,512]{0,1:T(8,128)}), f32[256,512]{0,1:T(8,128)}) %all-reduce.4.cloned.1.call-update) | async-done | bytes 524304 | tf_op jit(solution)/shard_map/psum | solution.py:106
  642.5 1.2 fusion.25
  643.6 1.2 fusion.29
  644.9 4.9 fusion.26
  649.8 1.3 dynamic-slice
  651.7 683.5 %all-reduce.6.cloned.1.call-done = f32[128,8192]{1,0:T(8,128)} async-done(((f32[128,8192]{1,0:T(8,128)}), f32[128,8192]{1,0:T(8,128)}) %all-reduce.6.cloned.1.call-update) | async-done | bytes 4194320
  1335.2 1.1 multiply_reduce_fusion.1
  1336.4 0.6 dynamic_slice.7
  1336.9 47.7 %psum.23 = f32[2]{0:T(128)S(1)} all-reduce(f32[2]{0:T(128)S(1)} %multiply_reduce_fusion.1), channel_id=1, replica_groups=mesh['img'=64,'tpl'=4,'pix'=2] {'pix'}, use_global_device_ids=true, to_apply=%region_10.11 | all-reduce | flops 2 | bytes 16 | tf_op jit(solution)/shard_map/psum | solution.py:124
  1384.7 1.0 multiply_bitcast_fusion
  1385.7 0.6 copy.21
  (28 shorter events, 0.4 us)
Async XLA Ops:
  7.2 3.3 copy-start
  7.2 326.1 %all-gather.6.cloned.1.call-start = ((), (), s32[]{:S(2)}) async-start(), calls=%async_computation.2 | async-start | bytes 2129920 | tf_op jit(solution)/shard_map/all_gather | solution.py:88
  12.5 4.9 copy-start.2
  17.4 523.5 %all-gather.4.cloned.1.call-start = ((), (), s32[]{:S(2)}) async-start(), calls=%async_computation | async-start | bytes 5242880 | tf_op jit(solution)/shard_map/all_gather | solution.py:93
  19.2 623.3 %all-reduce.4.cloned.1.call-start = ((), (), s32[]{:S(2)}) async-start(), calls=%async_computation.1 | async-start | bytes 1048576 | tf_op jit(solution)/shard_map/psum | solution.py:106
  336.0 209.6 %copy-start.3 = (f32[256]{0:T(256)S(1)}, f32[256]{0:T(256)}, u32[]{:S(2)}) copy-start(f32[256]{0:T(256)} %param.19) | copy-start | bytes 3076
  336.0 209.6 %copy-start.4 = (s32[256]{0:T(256)S(1)}, s32[256]{0:T(256)}, u32[]{:S(2)}) copy-start(s32[256]{0:T(256)} %param.18) | copy-start | bytes 3076
  544.6 0.8 copy-start.1
  545.5 789.7 %all-reduce.6.cloned.1.call-start = ((), (), s32[]{:S(2)}) async-start(), calls=%async_computation.3 | async-start | bytes 8388608
Sparse Core Ops, SparseCore 0:
  17.5 315.6 all-gather.5
  335.3 205.4 all-gather.3
  545.6 96.7 all-reduce.3
  649.9 685.2 all-reduce.5
where the time goes:
time: 1390 us
  waiting for transfers between devices  1280 us (92%)
  blocking collectives  66.1 us (5%)
  between operations  14.6 us (1%)
    unnamed x5, waiting for transfers between devices  684 us
    all_gather x1, waiting for transfers between devices, on_device(): templates = lax.all_gather(own_rendered, 'img', axis=0, tiled=True)  314 us
    all_gather x1, waiting for transfers between devices, on_device(): group_images = lax.all_gather(flat_rows, 'tpl', axis=0, tiled=True)  205 us
    psum x1, waiting for transfers between devices, on_device(): lax.psum((score_block, norm_block), ('tpl', 'pix'))  77.6 us
    psum x1, blocking collectives, on_device(): full_squares = lax.psum(part_squares, 'pix')  47.7 us
  transfers between devices with their start and end apart: 4, of which 4 were waited for; matrix products, arithmetic and copies ran while one was open for 0% of the time, Pallas kernels for 0%

commit v1 on v0

--- a/solution.py
+++ b/solution.py
@@ -85,7 +85,9 @@
     )(own_coords, own_angles)
     rendered_count = own_rendered.shape[0]
     own_rendered = own_rendered.astype(jnp.bfloat16).reshape(rendered_count, pixel_count)
-    templates = lax.all_gather(own_rendered, "img", axis=0, tiled=True)
+    templates = jnp.concatenate(
+        lax.all_to_all(jnp.stack([own_rendered] * lax.axis_size("img")), "img", 0, 0), axis=0
+    )
     tpl_dev = templates.shape[0]
     part_norms = jnp.sum(jnp.square(templates.astype(jnp.float32)), axis=1)
     precision_rows = group_lookup(group_ids, group_prec)

time: 1390 us -> 1070 us (0.77)
  waiting for transfers between devices: 1280 us -> 927 us
  blocking collectives: 66.1 us -> 82.6 us
    all_gather x1 -> x0, waiting for transfers between devices: 314 us -> none  [on_device(): templates = lax.all_gather(own_rendered, 'img', axis=0, tiled=True)]
    all_gather x1, waiting for transfers between devices: 205 us -> 0.01 us  [on_device(): group_images = lax.all_gather(flat_rows, 'tpl', axis=0, tiled=True)]
    all_to_all x0 -> x1, waiting for transfers between devices: none -> 141 us  [on_device(): lax.all_to_all(jnp.stack([own_rendered] * lax.axis_size('img')), 'img', 0...]
    psum x1, waiting for transfers between devices: 77.6 us -> 102 us  [on_device(): lax.psum((score_block, norm_block), ('tpl', 'pix'))]
    psum x1, blocking collectives: 18.4 us -> 34.9 us  [on_device(): lax.psum((score_block, norm_block), ('tpl', 'pix'))]
    unnamed x5 -> x4, waiting for transfers between devices: 684 us -> 684 us
  transfers between devices with their start and end apart: 4 -> 4, of which waited for: 4 -> 3; matrix products, arithmetic and copies ran while one was open for 0% -> 1% of each run, Pallas kernels for 0% -> 0%
where the time goes in v1:
time: 1070 us
  waiting for transfers between devices  927 us (87%)
  blocking collectives  82.6 us (8%)
  between operations  14.6 us (1%)
  local copies, waits for them, and re-layouts  13.5 us (1%)
  matrix products  13.5 us (1%)
  starting transfers between devices  12.9 us (1%)
    unnamed x4, waiting for transfers between devices  684 us
    all_to_all x1, waiting for transfers between devices, on_device(): lax.all_to_all(jnp.stack([own_rendered] * lax.axis_size('img')), 'img', 0...  141 us
    psum x1, waiting for transfers between devices, on_device(): lax.psum((score_block, norm_block), ('tpl', 'pix'))  102 us
    psum x1, blocking collectives, on_device(): full_squares = lax.psum(part_squares, 'pix')  47.7 us
    psum x1, blocking collectives, on_device(): lax.psum((score_block, norm_block), ('tpl', 'pix'))  34.9 us
  transfers between devices with their start and end apart: 4, of which 3 were waited for; matrix products, arithmetic and copies ran while one was open for 1% of the time, Pallas kernels for 0%

profile of v1, /device:TPU:1, one launch (start us, length us, event | category | flops | bytes accessed | tf_op | source)
XLA Modules:
  0.0 1073.7 jit_solution(3991209022586128116)
XLA Ops:
  7.2 0.7 compare_and_fusion
  7.9 0.7 compare_select_fusion
  8.6 0.8 copy.23
  9.4 0.6 gather_fusion
  10.1 0.3 add_reduce_fusion.1
  10.4 0.9 select_reduce_fusion.2
  11.3 0.9 gather_fusion.1
  12.5 4.2 fusion.21
  16.7 3.4 stack.3
  20.1 12.5 %all-to-all-start = ((bf16[64,2,8192]{2,1,0:T(2,128)(2,1)}), bf16[64,2,8192]{2,1,0:T(2,128)(2,1)S(1)}, u32[]{:S(2)}, u32[]{:S(2)}) async-start(bf16[64,2,8192]{2,1,0:T(2,128)(2,1)} %stack.3), calls=%async_computation | async-start | bytes 4194304 | tf_op jit(solution)/shard_map/all_to_all | solution.py:89
  32.7 1.7 copy.33
  34.5 141.3 %all-to-all-done = bf16[64,2,8192]{2,1,0:T(2,128)(2,1)S(1)} async-done(((bf16[64,2,8192]{2,1,0:T(2,128)(2,1)}), bf16[64,2,8192]{2,1,0:T(2,128)(2,1)S(1)}, u32[]{:S(2)}, u32[]{:S(2)}) %all-to-all-start) | async-done | bytes 2097184 | tf_op jit(solution)/shard_map/all_to_all | solution.py:89
  175.8 2.2 reshape.184
  178.1 4.4 fusion.15
  182.5 0.8 copy-done.1
  183.3 0.2 all-reduce.6.cloned.1.call-start
  183.6 0.2 select_reduce_fusion
  183.8 2.3 multiply_reduce_fusion
  186.1 0.1 reduce_sum.60
  186.3 0.2 dynamic_update_slice.7
  186.5 34.9 %psum.22 = f32[512]{0:T(512)S(1)} all-reduce(f32[512]{0:T(512)S(1)} %dynamic_update_slice.7), channel_id=1, replica_groups=mesh['img'=64,'tpl'=4,'pix'=2] {'tpl','pix'}, use_global_device_ids=true, to_apply=%region_5.6 | all-reduce | flops 512 | bytes 4096 | tf_op jit(solution)/shard_map/psum | solution.py:108
  221.4 101.6 %all-reduce.4.cloned.1.call-done = f32[256,512]{0,1:T(8,128)} async-done(((f32[256,512]{0,1:T(8,128)}), f32[256,512]{0,1:T(8,128)}) %all-reduce.4.cloned.1.call-update) | async-done | bytes 524304 | tf_op jit(solution)/shard_map/psum | solution.py:108
  323.1 1.2 fusion.30
  324.3 1.2 fusion.34
  325.5 4.9 fusion.31
  330.4 1.3 dynamic-slice
  332.3 683.8 %all-reduce.6.cloned.1.call-done = f32[128,8192]{1,0:T(8,128)} async-done(((f32[128,8192]{1,0:T(8,128)}), f32[128,8192]{1,0:T(8,128)}) %all-reduce.6.cloned.1.call-update) | async-done | bytes 4194320
  1016.1 1.1 multiply_reduce_fusion.1
  1017.2 0.6 dynamic_slice.7
  1017.8 47.7 %psum.23 = f32[2]{0:T(128)S(1)} all-reduce(f32[2]{0:T(128)S(1)} %multiply_reduce_fusion.1), channel_id=1, replica_groups=mesh['img'=64,'tpl'=4,'pix'=2] {'pix'}, use_global_device_ids=true, to_apply=%region_10.11 | all-reduce | flops 2 | bytes 16 | tf_op jit(solution)/shard_map/psum | solution.py:126
  1065.5 1.0 multiply_bitcast_fusion
  1066.6 0.6 copy.34
  (30 shorter events, 0.7 us)
Async XLA Ops:
  7.2 4.1 copy-start
  16.7 16.0 %copy-start.2 = (bf16[64,64,128]{2,1,0:T(8,128)(2,1)S(1)}, bf16[64,64,128]{2,1,0:T(8,128)(2,1)}, u32[]{:S(2)}) copy-start(bf16[64,64,128]{2,1,0:T(8,128)(2,1)} %param.10) | copy-start | bytes 3145732
  20.1 155.8 %all-to-all-start = ((bf16[64,2,8192]{2,1,0:T(2,128)(2,1)}), bf16[64,2,8192]{2,1,0:T(2,128)(2,1)S(1)}, u32[]{:S(2)}, u32[]{:S(2)}) async-start(bf16[64,2,8192]{2,1,0:T(2,128)(2,1)} %stack.3), calls=%async_computation | async-start | bytes 4194304 | tf_op jit(solution)/shard_map/all_to_all | solution.py:89
  32.6 145.4 %all-gather.2.cloned.1.call-start = ((), (), s32[]{:S(2)}) async-start(), calls=%async_computation.1 | async-start | bytes 5242880 | tf_op jit(solution)/shard_map/all_gather | solution.py:95
  34.4 288.6 %all-reduce.4.cloned.1.call-start = ((), (), s32[]{:S(2)}) async-start(), calls=%async_computation.2 | async-start | bytes 1048576 | tf_op jit(solution)/shard_map/psum | solution.py:108
  178.1 5.5 copy-start.3
  178.1 5.5 copy-start.4
  182.5 0.8 copy-start.1
  183.3 832.8 %all-reduce.6.cloned.1.call-start = ((), (), s32[]{:S(2)}) async-start(), calls=%async_computation.3 | async-start | bytes 8388608
Sparse Core Ops, SparseCore 0:
  35.6 127.9 all-gather.1
  183.4 139.5 all-reduce.3
  330.5 685.5 all-reduce.5
